TPU v7x, 32 devices: a whole 2x2x4 slice. The times are simulated.
32 devices in a mesh: comp: 2 (over x), lat: 4 (over y, core), lon: 4 (over z).
Axes of the slice: x: 2, y: 2, z: 4, core: 2. Of those that a mesh axis runs over, the one named last changes fastest.
Arguments:
- state: float32 [2, 12, 64, 512], P('comp', None, 'lat', 'lon'), may hold values from -6 to 6
- prev_surface: float32 [2, 64, 512], P(None, 'lat', 'lon'), may hold values from -6 to 6
- mixing: float32 [2, 11, 64, 512], P('comp', None, 'lat', 'lon'), may hold values from 0.1 to 3
- velocity: float32 [2, 2, 64, 512], P('comp', None, 'lat', 'lon'), may hold values from -0.3 to 0.3
- coupling: float32 [2, 64, 512], P('comp', 'lat', 'lon'), may hold values from 0.1 to 1
- sea_mask: int32 [2, 64, 512], P('comp', 'lat', 'lon'), may hold values 0 or 1
- interp_index: int32 [2, 4, 64, 512], P('comp', None, 'lat', 'lon'), may hold values from 0 to 2047
- interp_weight: float32 [2, 4, 64, 512], P('comp', None, 'lat', 'lon'), may hold values from 0.05 to 0.45
Outputs:
- new_state: float32 [2, 12, 64, 512], P('comp', None, 'lat', 'lon')
- surface_series: float32 [2, 2, 64, 512], P('comp', None, 'lat', 'lon')
Inputs may be any that keep to these rules, and one draw needn't show every extreme that they name: `interp_index`: A tile index, r * 128 + c, of a cell in the same latitude-longitude tile.
All inputs are finite; a program needn't handle non-finite values. No bound on the sum of `sea_mask` on one device may be relied on, other than what follows from the above.
Results may differ from a plain program's by a relative error of at most 0.0001.
Values sent between devices are 32-bit elements; how exact they have to be, the bound alone decides.
A program may use at most 64 MiB of HBM per device.

v0:
```python
import jax
import jax.numpy as jnp
from jax import lax
from jax.sharding import PartitionSpec as P

NSTEP = 2


smoothing = 0.15


def extended(shard, sides, width, wrap):
    for axis, dim in sides:
        size, length = (lax.axis_size(axis), shard.shape[dim])
        up = [(i, (i + 1) % size) for i in range(size if wrap else size - 1)]
        down = [(j, i) for i, j in up]
        last = lax.slice_in_dim(shard, length - width, length, axis=dim)
        initial = lax.slice_in_dim(shard, 0, width, axis=dim)
        before = lax.ppermute(last, axis, up)
        after = lax.ppermute(initial, axis, down)
        shard = jnp.concatenate([before, shard, after], axis=dim)
    return shard


def passed_along(value, axis, steps):
    count = lax.axis_size(axis)
    initial, last = (max(0, -steps), min(count, count - steps))
    return lax.ppermute(value, axis, [(source, source + steps) for source in range(initial, last)])


def stencil(field, lat_padded, lon_padded, east_speed, north_speed):
    lat_slope = (
        lat_padded[:, 0:-4]
        - 8.0 * lat_padded[:, 1:-3]
        + 8.0 * lat_padded[:, 3:-1]
        - lat_padded[:, 4:]
    ) / 12.0
    lon_slope = (
        lon_padded[:, :, 0:-4]
        - 8.0 * lon_padded[:, :, 1:-3]
        + 8.0 * lon_padded[:, :, 3:-1]
        - lon_padded[:, :, 4:]
    ) / 12.0
    lat_curve = lat_padded[:, 1:-3] + lat_padded[:, 3:-1] - 2.0 * field
    lon_curve = lon_padded[:, :, 1:-3] + lon_padded[:, :, 3:-1] - 2.0 * field
    return (
        field
        + smoothing * (lat_curve + lon_curve)
        - east_speed * lon_slope
        - north_speed * lat_slope
    )


def column_solve(rhs, mixing):
    levels = rhs.shape[0]
    nothing = jnp.zeros_like(rhs[0])
    ratios = []
    values = []
    for level in range(levels):
        lower = mixing[level - 1] if level > 0 else nothing
        upper = mixing[level] if level < levels - 1 else nothing
        pivot = 1.0 + lower + upper
        source = rhs[level]
        if level > 0:
            pivot = pivot + lower * ratios[-1]
            source = source + lower * values[-1]
        ratios.append(-upper / pivot)
        values.append(source / pivot)
    result = [values[-1]]
    for level in range(levels - 2, -1, -1):
        result.insert(0, values[level] - ratios[level] * result[0])
    return jnp.stack(result)


def regrid_local(source, index, weight):
    flat = source.reshape(-1)
    picked = jnp.take(flat, index.reshape(index.shape[0], -1), axis=0).reshape(index.shape)
    return jnp.sum(weight * picked, axis=0)


def padded_rims(field):
    lat_padded = extended(field, (("lat", 1),), 2, False)
    lon_padded = extended(field, (("lon", 2),), 2, True)
    return (lat_padded, lon_padded)


def per_device(
    state, prev_surface, mixing, velocity, coupling, sea_mask, interp_index, interp_weight
):
    is_atmosphere = lax.axis_index("comp") == 0
    field = state[0]
    column_mixing = mixing[0]
    east_speed = velocity[0, 0]
    north_speed = velocity[0, 1]
    exchange_rate = coupling[0] * sea_mask[0].astype(jnp.float32)
    index = interp_index[0]
    weight = interp_weight[0]
    received = jnp.zeros_like(field[0])
    first_series = []
    second_series = []
    for round_index in range(NSTEP + 1):
        if round_index < NSTEP:
            own_source = prev_surface[round_index]
        else:
            own_source = jnp.zeros_like(received)
        source = jnp.where(is_atmosphere, own_source, received)
        partner = regrid_local(source, index, weight)
        lat_padded, lon_padded = padded_rims(field)
        moved = stencil(field, lat_padded, lon_padded, east_speed, north_speed)
        forcing = jnp.where(
            is_atmosphere, exchange_rate * (partner - field[0]), exchange_rate * partner
        )
        moved = moved.at[0].add(forcing)
        solved = column_solve(moved, column_mixing)
        surface_now = jnp.where(is_atmosphere, forcing, solved[0])
        active = jnp.where(is_atmosphere, round_index < NSTEP, round_index >= 1)
        field = jnp.where(active, solved, field)
        if round_index < NSTEP:
            first_series.append(surface_now)
            received = passed_along(surface_now, "comp", 1)
        if round_index >= 1:
            second_series.append(surface_now)
    series = jnp.where(is_atmosphere, jnp.stack(first_series), jnp.stack(second_series))
    return (field[None], series[None])


def solution(mesh):
    in_specs = (
        P("comp", None, "lat", "lon"),
        P(None, "lat", "lon"),
        P("comp", None, "lat", "lon"),
        P("comp", None, "lat", "lon"),
        P("comp", "lat", "lon"),
        P("comp", "lat", "lon"),
        P("comp", None, "lat", "lon"),
        P("comp", None, "lat", "lon"),
    )
    out_specs = (P("comp", None, "lat", "lon"), P("comp", None, "lat", "lon"))
    return jax.shard_map(
        per_device, mesh=mesh, in_specs=in_specs, out_specs=out_specs, check_vma=False
    )
```

profile of v0, /device:TPU:0, one launch (start us, length us, event | category | flops | bytes accessed | tf_op | source)
XLA Modules:
  0.0 176.6 jit_solution(17240412378446014431)
XLA Ops:
  0.6 1.1 fusion.270
  1.8 3.1 %collective-permute-start.2 = (f32[12,16,2]{2,1,0:T(8,128)S(1)}, f32[12,16,2]{2,1,0:T(8,128)S(1)}, u32[]{:S(2)}, u32[]{:S(2)}) collective-permute-start(f32[12,16,2]{2,1,0:T(8,128)S(1)} %get-tuple-element.129), channel_id=1, source_target_pairs={{0,1},{1,2},{2,3},{3,0},{4,5},{5,6},{6,7},{7,4},{8,9},{9,10},{10,1... | collective-permute-start | bytes 4616 | tf_op jit(solution)/shard_map/ppermute | solution.py:19
  4.8 2.1 %collective-permute-start.3 = (f32[12,16,2]{2,1,0:T(8,128)S(1)}, f32[12,16,2]{2,1,0:T(8,128)S(1)}, u32[]{:S(2)}, u32[]{:S(2)}) collective-permute-start(f32[12,16,2]{2,1,0:T(8,128)S(1)} %get-tuple-element.130), channel_id=1, source_target_pairs={{1,0},{2,1},{3,2},{0,3},{5,4},{6,5},{7,6},{4,7},{9,8},{10,9},{11,1... | collective-permute-start | bytes 4616 | tf_op jit(solution)/shard_map/ppermute | solution.py:20
  7.0 1.5 collective-permute-start
  8.4 1.3 collective-permute-start.1
  9.8 0.7 copy-done.4
  10.5 45.5 %gather_fusion = f32[8192]{0:T(1024)S(1)} fusion(f32[2048]{0:T(1024)S(1)} %select_bitcast_fusion.7, s32[8192]{0:T(1024)S(1)} %broadcast_clamp_fusion), kind=kCustom, calls=%fused_computation.clone | custom fusion | bytes 98304 | tf_op jit(solution)/shard_map/jit(_take)/gather | solution.py:77
  56.1 0.7 copy-done.2
  56.9 0.3 fusion.34
  57.2 0.6 copy-done
  57.8 0.1 fusion.143
  57.9 0.1 fusion.161
  58.0 0.1 select_bitcast_fusion.5
  58.3 0.1 fusion.268
  58.4 3.4 %collective-permute-start.8 = (f32[16,128]{1,0:T(8,128)S(1)}, f32[16,128]{1,0:T(8,128)S(1)}, u32[]{:S(2)}, u32[]{:S(2)}) collective-permute-start(f32[16,128]{1,0:T(8,128)S(1)} %get-tuple-element.90), channel_id=1, source_target_pairs={{0,16},{1,17},{2,18},{3,19},{4,20},{5,21},{6,22},{7,23},{8,24},{9,... | collective-permute-start | bytes 24584 | tf_op jit(solution)/shard_map/ppermute | solution.py:28
  61.9 3.8 %collective-permute-start.7 = (f32[12,16,2]{2,1,0:T(8,128)S(1)}, f32[12,16,2]{2,1,0:T(8,128)S(1)}, u32[]{:S(2)}, u32[]{:S(2)}) collective-permute-start(f32[12,16,2]{2,1,0:T(8,128)S(1)} %get-tuple-element.126), channel_id=1, source_target_pairs={{1,0},{2,1},{3,2},{0,3},{5,4},{6,5},{7,6},{4,7},{9,8},{10,9},{11,1... | collective-permute-start | bytes 4616 | tf_op jit(solution)/shard_map/ppermute | solution.py:20
  65.7 3.9 %collective-permute-start.4 = (f32[12,2,128]{2,1,0:T(2,128)S(1)}, f32[12,2,128]{2,1,0:T(2,128)S(1)}, u32[]{:S(2)}, u32[]{:S(2)}) collective-permute-start(f32[12,2,128]{2,1,0:T(2,128)S(1)} %get-tuple-element.127), channel_id=1, source_target_pairs={{0,4},{4,8},{8,12},{1,5},{5,9},{9,13},{2,6},{6,10},{10,14},{3,7},{... | collective-permute-start | bytes 36872 | tf_op jit(solution)/shard_map/ppermute | solution.py:19
  69.6 1.3 collective-permute-start.5
  70.9 45.5 %gather_fusion.1 = f32[8192]{0:T(1024)S(1)} fusion(f32[2048]{0:T(1024)S(1)} %fusion.144, s32[8192]{0:T(1024)S(1)} %broadcast_clamp_fusion), kind=kCustom, calls=%fused_computation.1.clone | custom fusion | bytes 98304 | tf_op jit(solution)/shard_map/jit(_take)/gather | solution.py:77
  116.6 0.3 fusion.24
  116.8 0.1 fusion.88
  117.0 0.1 select_bitcast_fusion.4
  117.2 0.1 fusion.266
  117.4 1.6 collective-permute-start.13
  119.0 3.8 %collective-permute-start.12 = (f32[12,16,2]{2,1,0:T(8,128)S(1)}, f32[12,16,2]{2,1,0:T(8,128)S(1)}, u32[]{:S(2)}, u32[]{:S(2)}) collective-permute-start(f32[12,16,2]{2,1,0:T(8,128)S(1)} %get-tuple-element.122), channel_id=1, source_target_pairs={{1,0},{2,1},{3,2},{0,3},{5,4},{6,5},{7,6},{4,7},{9,8},{10,9},{11,1... | collective-permute-start | bytes 4616 | tf_op jit(solution)/shard_map/ppermute | solution.py:20
  122.8 1.3 collective-permute-start.10
  124.1 4.9 %collective-permute-start.9 = (f32[12,2,128]{2,1,0:T(2,128)S(1)}, f32[12,2,128]{2,1,0:T(2,128)S(1)}, u32[]{:S(2)}, u32[]{:S(2)}) collective-permute-start(f32[12,2,128]{2,1,0:T(2,128)S(1)} %get-tuple-element.123), channel_id=1, source_target_pairs={{0,4},{4,8},{8,12},{1,5},{5,9},{9,13},{2,6},{6,10},{10,14},{3,7},{... | collective-permute-start | bytes 36872 | tf_op jit(solution)/shard_map/ppermute | solution.py:19
  129.2 45.5 %gather_fusion.2 = f32[8192]{0:T(1024)S(1)} fusion(f32[2048]{0:T(1024)S(1)} %select_bitcast_fusion.6, s32[8192]{0:T(1024)S(1)} %broadcast_clamp_fusion), kind=kCustom, calls=%fused_computation.2.clone | custom fusion | bytes 98304 | tf_op jit(solution)/shard_map/jit(_take)/gather | solution.py:77
  174.8 0.3 fusion.14
  175.1 0.1 select_bitcast_fusion.3
  175.3 0.6 maximum_select_fusion
  176.0 0.7 broadcast_select_fusion.1
  (99 shorter events, 0.8 us)
Async XLA Ops:
  0.6 6.3 %copy-start.1 = (f32[1,12,16,128]{3,2,1,0:T(8,128)S(1)}, f32[1,12,16,128]{3,2,1,0:T(8,128)}, u32[]{:S(2)}) copy-start(f32[1,12,16,128]{3,2,1,0:T(8,128)} %param.16) | copy-start | bytes 294916
  1.8 55.1 %collective-permute-start.2 = (f32[12,16,2]{2,1,0:T(8,128)S(1)}, f32[12,16,2]{2,1,0:T(8,128)S(1)}, u32[]{:S(2)}, u32[]{:S(2)}) collective-permute-start(f32[12,16,2]{2,1,0:T(8,128)S(1)} %get-tuple-element.129), channel_id=1, source_target_pairs={{0,1},{1,2},{2,3},{3,0},{4,5},{5,6},{6,7},{7,4},{8,9},{9,10},{10,1... | collective-permute-start | bytes 4616 | tf_op jit(solution)/shard_map/ppermute | solution.py:19
  4.8 4.9 %copy-start.5 = (f32[1,2,16,128]{3,2,1,0:T(8,128)S(1)}, f32[1,2,16,128]{3,2,1,0:T(8,128)}, u32[]{:S(2)}) copy-start(f32[1,2,16,128]{3,2,1,0:T(8,128)} %param.19) | copy-start | bytes 49156
  4.8 52.0 %collective-permute-start.3 = (f32[12,16,2]{2,1,0:T(8,128)S(1)}, f32[12,16,2]{2,1,0:T(8,128)S(1)}, u32[]{:S(2)}, u32[]{:S(2)}) collective-permute-start(f32[12,16,2]{2,1,0:T(8,128)S(1)} %get-tuple-element.130), channel_id=1, source_target_pairs={{1,0},{2,1},{3,2},{0,3},{5,4},{6,5},{7,6},{4,7},{9,8},{10,9},{11,1... | collective-permute-start | bytes 4616 | tf_op jit(solution)/shard_map/ppermute | solution.py:20
  7.0 2.8 %copy-start.3 = (s32[1,4,16,128]{3,2,1,0:T(8,128)S(1)}, s32[1,4,16,128]{3,2,1,0:T(8,128)}, u32[]{:S(2)}) copy-start(s32[1,4,16,128]{3,2,1,0:T(8,128)} %param.22) | copy-start | bytes 98308
  7.0 49.9 %collective-permute-start = (f32[12,2,128]{2,1,0:T(2,128)S(1)}, f32[12,2,128]{2,1,0:T(2,128)S(1)}, u32[]{:S(2)}, u32[]{:S(2)}) collective-permute-start(f32[12,2,128]{2,1,0:T(2,128)S(1)} %get-tuple-element.131), channel_id=1, source_target_pairs={{0,4},{4,8},{8,12},{1,5},{5,9},{9,13},{2,6},{6,10},{10,14},{3,7},{... | collective-permute-start | bytes 36872 | tf_op jit(solution)/shard_map/ppermute | solution.py:19
  8.4 48.5 %collective-permute-start.1 = (f32[12,2,128]{2,1,0:T(2,128)S(1)}, f32[12,2,128]{2,1,0:T(2,128)S(1)}, u32[]{:S(2)}, u32[]{:S(2)}) collective-permute-start(f32[12,2,128]{2,1,0:T(2,128)S(1)} %get-tuple-element.132), channel_id=1, source_target_pairs={{4,0},{8,4},{12,8},{5,1},{9,5},{13,9},{6,2},{10,6},{14,10},{7,3},{... | collective-permute-start | bytes 36872 | tf_op jit(solution)/shard_map/ppermute | solution.py:20
  9.8 0.7 copy-start.4
  56.1 0.8 copy-start.2
  56.9 0.9 copy-start
  56.9 0.9 copy-start.6
  56.9 0.9 copy-start.7
  58.4 12.5 %collective-permute-start.8 = (f32[16,128]{1,0:T(8,128)S(1)}, f32[16,128]{1,0:T(8,128)S(1)}, u32[]{:S(2)}, u32[]{:S(2)}) collective-permute-start(f32[16,128]{1,0:T(8,128)S(1)} %get-tuple-element.90), channel_id=1, source_target_pairs={{0,16},{1,17},{2,18},{3,19},{4,20},{5,21},{6,22},{7,23},{8,24},{9,... | collective-permute-start | bytes 24584 | tf_op jit(solution)/shard_map/ppermute | solution.py:28
  61.8 54.7 %collective-permute-start.6 = (f32[12,16,2]{2,1,0:T(8,128)S(1)}, f32[12,16,2]{2,1,0:T(8,128)S(1)}, u32[]{:S(2)}, u32[]{:S(2)}) collective-permute-start(f32[12,16,2]{2,1,0:T(8,128)S(1)} %get-tuple-element.125), channel_id=1, source_target_pairs={{0,1},{1,2},{2,3},{3,0},{4,5},{5,6},{6,7},{7,4},{8,9},{9,10},{10,1... | collective-permute-start | bytes 4616 | tf_op jit(solution)/shard_map/ppermute | solution.py:19
  61.9 54.7 %collective-permute-start.7 = (f32[12,16,2]{2,1,0:T(8,128)S(1)}, f32[12,16,2]{2,1,0:T(8,128)S(1)}, u32[]{:S(2)}, u32[]{:S(2)}) collective-permute-start(f32[12,16,2]{2,1,0:T(8,128)S(1)} %get-tuple-element.126), channel_id=1, source_target_pairs={{1,0},{2,1},{3,2},{0,3},{5,4},{6,5},{7,6},{4,7},{9,8},{10,9},{11,1... | collective-permute-start | bytes 4616 | tf_op jit(solution)/shard_map/ppermute | solution.py:20
  65.7 50.9 %collective-permute-start.4 = (f32[12,2,128]{2,1,0:T(2,128)S(1)}, f32[12,2,128]{2,1,0:T(2,128)S(1)}, u32[]{:S(2)}, u32[]{:S(2)}) collective-permute-start(f32[12,2,128]{2,1,0:T(2,128)S(1)} %get-tuple-element.127), channel_id=1, source_target_pairs={{0,4},{4,8},{8,12},{1,5},{5,9},{9,13},{2,6},{6,10},{10,14},{3,7},{... | collective-permute-start | bytes 36872 | tf_op jit(solution)/shard_map/ppermute | solution.py:19
  69.6 47.0 %collective-permute-start.5 = (f32[12,2,128]{2,1,0:T(2,128)S(1)}, f32[12,2,128]{2,1,0:T(2,128)S(1)}, u32[]{:S(2)}, u32[]{:S(2)}) collective-permute-start(f32[12,2,128]{2,1,0:T(2,128)S(1)} %get-tuple-element.128), channel_id=1, source_target_pairs={{4,0},{8,4},{12,8},{5,1},{9,5},{13,9},{6,2},{10,6},{14,10},{7,3},{... | collective-permute-start | bytes 36872 | tf_op jit(solution)/shard_map/ppermute | solution.py:20
  117.4 11.8 %collective-permute-start.13 = (f32[16,128]{1,0:T(8,128)S(1)}, f32[16,128]{1,0:T(8,128)S(1)}, u32[]{:S(2)}, u32[]{:S(2)}) collective-permute-start(f32[16,128]{1,0:T(8,128)S(1)} %fusion.88), channel_id=1, source_target_pairs={{0,16},{1,17},{2,18},{3,19},{4,20},{5,21},{6,22},{7,23},{8,24},{9,... | collective-permute-start | bytes 24584 | tf_op jit(solution)/shard_map/ppermute | solution.py:28
  118.9 55.8 %collective-permute-start.11 = (f32[12,16,2]{2,1,0:T(8,128)S(1)}, f32[12,16,2]{2,1,0:T(8,128)S(1)}, u32[]{:S(2)}, u32[]{:S(2)}) collective-permute-start(f32[12,16,2]{2,1,0:T(8,128)S(1)} %get-tuple-element.121), channel_id=1, source_target_pairs={{0,1},{1,2},{2,3},{3,0},{4,5},{5,6},{6,7},{7,4},{8,9},{9,10},{10,1... | collective-permute-start | bytes 4616 | tf_op jit(solution)/shard_map/ppermute | solution.py:19
  119.0 55.8 %collective-permute-start.12 = (f32[12,16,2]{2,1,0:T(8,128)S(1)}, f32[12,16,2]{2,1,0:T(8,128)S(1)}, u32[]{:S(2)}, u32[]{:S(2)}) collective-permute-start(f32[12,16,2]{2,1,0:T(8,128)S(1)} %get-tuple-element.122), channel_id=1, source_target_pairs={{1,0},{2,1},{3,2},{0,3},{5,4},{6,5},{7,6},{4,7},{9,8},{10,9},{11,1... | collective-permute-start | bytes 4616 | tf_op jit(solution)/shard_map/ppermute | solution.py:20
  122.8 52.0 %collective-permute-start.10 = (f32[12,2,128]{2,1,0:T(2,128)S(1)}, f32[12,2,128]{2,1,0:T(2,128)S(1)}, u32[]{:S(2)}, u32[]{:S(2)}) collective-permute-start(f32[12,2,128]{2,1,0:T(2,128)S(1)} %get-tuple-element.124), channel_id=1, source_target_pairs={{4,0},{8,4},{12,8},{5,1},{9,5},{13,9},{6,2},{10,6},{14,10},{7,3},{... | collective-permute-start | bytes 36872 | tf_op jit(solution)/shard_map/ppermute | solution.py:20
  124.1 50.7 %collective-permute-start.9 = (f32[12,2,128]{2,1,0:T(2,128)S(1)}, f32[12,2,128]{2,1,0:T(2,128)S(1)}, u32[]{:S(2)}, u32[]{:S(2)}) collective-permute-start(f32[12,2,128]{2,1,0:T(2,128)S(1)} %get-tuple-element.123), channel_id=1, source_target_pairs={{0,4},{4,8},{8,12},{1,5},{5,9},{9,13},{2,6},{6,10},{10,14},{3,7},{... | collective-permute-start | bytes 36872 | tf_op jit(solution)/shard_map/ppermute | solution.py:19
where the time goes:
time: 179 us; the launch traced here: 177 us
  local copies, waits for them, and re-layouts  140 us (78%)
  starting transfers between devices  32 us (18%)
  other arithmetic  2.96 us (2%)
    gather x6, local copies, waits for them, and re-layouts, regrid_local(): jnp.take(flat, index.reshape(index.shape[0], -1), axis=0)  137 us
    ppermute x6, starting transfers between devices, extended(): after = lax.ppermute(initial, axis, down)  13.6 us
    ppermute x6, starting transfers between devices, extended(): before = lax.ppermute(last, axis, up)  13.5 us
    ppermute x2, starting transfers between devices, passed_along(): lax.ppermute(value, axis, [(source, source + steps) for source in range(i...  4.97 us
  transfers between devices with their start and end apart: 14, of which 0 were waited for; matrix products, arithmetic and copies ran while one was open for 77% of the time, Pallas kernels for 0%

commit v1 on v0

v1 whole, which is shorter than its diff:
```python
import functools

import jax
import jax.numpy as jnp
from jax import lax
from jax.experimental import pallas as pl
from jax.experimental.pallas import tpu as pltpu
from jax.sharding import PartitionSpec as P

SMOOTHING = 0.15
MESH = pl.DeviceIdType.MESH
PAD = 8
REACH = 2
SUB = 8


def lane_gather(values, lanes):
    return jnp.take_along_axis(values, lanes, axis=1, mode="promise_in_bounds")


def regrid(source, index, weight):
    points, rows, cols = index.shape
    shift = cols.bit_length() - 1
    parts = []
    for top in range(0, rows, SUB):
        where = [index[j, top : top + SUB, :] for j in range(points)]
        lanes = [lax.bitwise_and(w, cols - 1) for w in where]
        owners = [lax.shift_right_logical(w, shift) for w in where]
        picked = [jnp.zeros((SUB, cols), jnp.float32)] * points
        for row in range(rows):
            line = jnp.broadcast_to(source[row : row + 1, :], (SUB, cols))
            for j in range(points):
                picked[j] = jnp.where(owners[j] == row, lane_gather(line, lanes[j]), picked[j])
        total = weight[0, top : top + SUB, :] * picked[0]
        for j in range(1, points):
            total = total + weight[j, top : top + SUB, :] * picked[j]
        parts.append(total)
    return jnp.concatenate(parts, axis=0)


def kernel(
    sizes,
    state,
    prev,
    mixing,
    velocity,
    coupling,
    sea_mask,
    interp_index,
    interp_weight,
    new_state,
    series,
    ext,
    src,
    mix,
    vel,
    cpl,
    sea,
    idx,
    wgt,
    part,
    flux,
    y,
    lon_out,
    lon_in,
    in_sem,
    src_sem,
    lat_send,
    lat_recv,
    lon_send,
    lon_recv,
    flux_send,
    flux_recv,
):
    n_lat, n_lon, steps, levels, rows, cols = sizes
    comp, lat, lon = (lax.axis_index(a) for a in ("comp", "lat", "lon"))
    is_atmosphere = comp == 0
    is_ocean = comp != 0
    has_before = lat > 0
    has_after = lat < n_lat - 1
    before, after = {"lat": lat - 1}, {"lat": lat + 1}
    west, east = {"lon": lax.rem(lon + n_lon - 1, n_lon)}, {"lon": lax.rem(lon + 1, n_lon)}
    partner = {"comp": 1 - comp}
    own = pl.ds(PAD, rows)

    loads = [
        pltpu.make_async_copy(a, b, in_sem.at[i])
        for i, (a, b) in enumerate(
            (
                (state.at[0], ext.at[0, :, own, :]),
                (interp_index.at[0], idx),
                (interp_weight.at[0], wgt),
                (coupling.at[0], cpl),
                (sea_mask.at[0], sea),
                (velocity.at[0], vel),
                (mixing.at[0], mix),
            )
        )
    ]
    sources = [pltpu.make_async_copy(prev.at[s], src.at[s], src_sem.at[s]) for s in range(steps)]

    def remote(a, b, send, recv, device):
        return pltpu.make_async_remote_copy(
            src_ref=a, dst_ref=b, send_sem=send, recv_sem=recv, device_id=device, device_id_type=MESH
        )

    low, high = pl.ds(PAD, REACH), pl.ds(PAD + rows - REACH, REACH)
    halo_low, halo_high = pl.ds(PAD - REACH, REACH), pl.ds(PAD + rows, REACH)
    to_before, to_after, to_west, to_east, to_ocean = [], [], [], [], []
    for s in range(steps):
        to_before.append(
            remote(ext.at[s, :, low, :], ext.at[s, :, halo_high, :], lat_send.at[s, 0], lat_recv.at[s, 0], before)
        )
        to_after.append(
            remote(ext.at[s, :, high, :], ext.at[s, :, halo_low, :], lat_send.at[s, 1], lat_recv.at[s, 1], after)
        )
        to_west.append(remote(lon_out.at[s], lon_in.at[s, 0], lon_send.at[s, 0], lon_recv.at[s, 0], west))
        to_east.append(remote(lon_out.at[s], lon_in.at[s, 1], lon_send.at[s, 1], lon_recv.at[s, 1], east))
        to_ocean.append(remote(flux.at[s], src.at[s], flux_send.at[s], flux_recv.at[s], partner))

    barrier = pltpu.get_barrier_semaphore()

    @pl.when(has_before)
    def _():
        pl.semaphore_signal(barrier, inc=1, device_id=before, device_id_type=MESH)

    @pl.when(has_after)
    def _():
        pl.semaphore_signal(barrier, inc=1, device_id=after, device_id_type=MESH)

    for side in (west, east):
        pl.semaphore_signal(barrier, inc=1, device_id=side, device_id_type=MESH)

    @pl.when(is_ocean)
    def _():
        pl.semaphore_signal(barrier, inc=1, device_id=partner, device_id_type=MESH)

    @pl.when(is_atmosphere)
    def _():
        for copy in sources:
            copy.start()

    for copy in loads:
        copy.start()

    lane = lax.broadcasted_iota(jnp.int32, (rows, cols), 1)

    def pack(s):
        packed = jnp.zeros((rows, cols), jnp.float32)
        for level in range(levels):
            turned = pltpu.roll(ext[s, level, own, :], (4 * level + REACH) % cols, 1)
            packed = jnp.where((lane >= 4 * level) & (lane < 4 * level + 4), turned, packed)
        lon_out[s] = packed

    loads[0].wait()
    pack(0)
    nothing = jnp.zeros((steps, levels, REACH, cols), jnp.float32)

    @pl.when(jnp.logical_not(has_before))
    def _():
        ext[:, :, halo_low, :] = nothing

    @pl.when(jnp.logical_not(has_after))
    def _():
        ext[:, :, halo_high, :] = nothing

    for copy in loads[1:5]:
        copy.wait()
    rate = cpl[...] * sea[...].astype(jnp.float32)

    @pl.when(is_atmosphere)
    def _():
        sources[0].wait()
        part[0] = regrid(src.at[0], idx, wgt)
        flux[0] = rate * (part[0] - ext[0, 0, own, :])

    edges = has_before.astype(jnp.int32) + has_after.astype(jnp.int32)
    pl.semaphore_wait(barrier, 2 + edges + is_atmosphere.astype(jnp.int32))

    def send_halo(s):
        @pl.when(has_before)
        def _():
            to_before[s].start()

        @pl.when(has_after)
        def _():
            to_after[s].start()

        to_west[s].start()
        to_east[s].start()

    @pl.when(is_atmosphere)
    def _():
        to_ocean[0].start()

    send_halo(0)

    loads[5].wait()
    loads[6].wait()
    east_speed, north_speed = vel[0] * (1.0 / 12.0), vel[1] * (1.0 / 12.0)
    centre = 1.0 - 4.0 * SMOOTHING
    lon_m2, lon_m1 = -east_speed, SMOOTHING + 8.0 * east_speed
    lon_p1, lon_p2 = SMOOTHING - 8.0 * east_speed, east_speed
    lat_m2, lat_m1 = -north_speed, SMOOTHING + 8.0 * north_speed
    lat_p1, lat_p2 = SMOOTHING - 8.0 * north_speed, north_speed
    own_m2, own_m1 = jnp.where(lane < 2, 0.0, lon_m2), jnp.where(lane < 1, 0.0, lon_m1)
    own_p1 = jnp.where(lane >= cols - 1, 0.0, lon_p1)
    own_p2 = jnp.where(lane >= cols - 2, 0.0, lon_p2)
    place = lax.bitwise_and(lane, 3)
    rim = lax.bitwise_and(place + (cols - REACH), cols - 1)
    spread = lambda c, keep: jnp.where(keep, lane_gather(c, rim), 0.0)
    rim_p2 = spread(lon_p2, place < 2)
    rim_p1 = spread(lon_p1, place == 1)
    rim_m2 = spread(lon_m2, place >= 2)
    rim_m1 = spread(lon_m1, place == 2)
    on_rim = (lane < REACH) | (lane >= cols - REACH)

    inverse, ratio = [None] * levels, [None] * levels
    for level in range(levels - 1, -1, -1):
        pivot = 1.0
        if level < levels - 1:
            pivot = pivot + mix[level] * (1.0 - ratio[level + 1])
        if level > 0:
            pivot = pivot + mix[level - 1]
        inverse[level] = 1.0 / pivot
        if level > 0:
            ratio[level] = mix[level - 1] * inverse[level]

    def own_part(s):
        for level in range(levels):
            x = ext[s, level, own, :]
            y[level] = (
                centre * x
                + own_m2 * pltpu.roll(x, 2, 1)
                + own_m1 * pltpu.roll(x, 1, 1)
                + own_p1 * pltpu.roll(x, cols - 1, 1)
                + own_p2 * pltpu.roll(x, cols - 2, 1)
            )

    for s in range(steps):
        own_part(s)
        if s + 1 < steps:

            @pl.when(is_atmosphere)
            def _():
                sources[s + 1].wait()
                part[s + 1] = regrid(src.at[s + 1], idx, wgt)

        @pl.when(has_after)
        def _():
            to_before[s].wait_recv()

        @pl.when(has_before)
        def _():
            to_after[s].wait_recv()

        to_west[s].wait_recv()
        to_east[s].wait_recv()
        from_east, from_west = lon_in[s, 0], lon_in[s, 1]
        rims = (
            rim_p2 * pltpu.roll(from_east, cols - 2, 1)
            + rim_p1 * pltpu.roll(from_east, cols - 1, 1)
            + rim_m2 * pltpu.roll(from_west, 2, 1)
            + rim_m1 * pltpu.roll(from_west, 1, 1)
        )
        values = [None] * levels
        for level in range(levels - 1, -1, -1):
            total = (
                y[level]
                + lat_m2 * ext[s, level, pl.ds(PAD - 2, rows), :]
                + lat_m1 * ext[s, level, pl.ds(PAD - 1, rows), :]
                + lat_p1 * ext[s, level, pl.ds(PAD + 1, rows), :]
                + lat_p2 * ext[s, level, pl.ds(PAD + 2, rows), :]
                + jnp.where(on_rim, pltpu.roll(rims, (cols - REACH - 4 * level) % cols, 1), 0.0)
            )
            if level < levels - 1:
                total = total + mix[level] * values[level + 1]
            if level > 0:
                values[level] = total * inverse[level]
            else:
                y[0] = total

        @pl.when(is_ocean)
        def _():
            to_ocean[s].wait_recv()
            forcing = rate * regrid(src.at[s], idx, wgt)
            part[s] = forcing

        if s == 0:
            forcing = jnp.where(is_atmosphere, flux[0], part[0])
        else:
            forcing = jnp.where(is_atmosphere, flux[s], part[s])
        x = (y[0] + forcing) * inverse[0]
        series[0, s] = jnp.where(is_atmosphere, forcing, x)
        last = s + 1 == steps
        if not last:

            @pl.when(is_atmosphere)
            def _():
                flux[s + 1] = rate * (part[s + 1] - x)
                to_ocean[s + 1].start()

        for level in range(levels):
            if level > 0:
                x = values[level] + ratio[level] * x
            if last:
                new_state[0, level] = x
            else:
                ext[s + 1, level, own, :] = x
        if not last:
            pack(s + 1)
            send_halo(s + 1)

    for s in range(steps):

        @pl.when(is_atmosphere)
        def _():
            to_ocean[s].wait_send()

        @pl.when(has_before)
        def _():
            to_before[s].wait_send()

        @pl.when(has_after)
        def _():
            to_after[s].wait_send()

        to_west[s].wait_send()
        to_east[s].wait_send()


def per_device(n_lat, n_lon, state, prev, mixing, velocity, coupling, sea_mask, index, weight):
    levels, rows, cols = state.shape[1:]
    steps, points = prev.shape[0], index.shape[1]
    tile = (rows, cols)
    floats = lambda *lead: pltpu.VMEM(lead + tile, jnp.float32)
    dma = pltpu.SemaphoreType.DMA
    return pl.pallas_call(
        functools.partial(kernel, (n_lat, n_lon, steps, levels, rows, cols)),
        out_shape=(
            jax.ShapeDtypeStruct(state.shape, jnp.float32),
            jax.ShapeDtypeStruct((1, steps) + tile, jnp.float32),
        ),
        in_specs=[pl.BlockSpec(memory_space=pltpu.HBM)] * 8,
        out_specs=[pl.BlockSpec(memory_space=pltpu.VMEM)] * 2,
        scratch_shapes=[
            pltpu.VMEM((steps, levels, rows + 2 * PAD, cols), jnp.float32),
            floats(steps),
            floats(levels - 1),
            floats(2),
            floats(),
            pltpu.VMEM(tile, jnp.int32),
            pltpu.VMEM((points,) + tile, jnp.int32),
            floats(points),
            floats(steps),
            floats(steps),
            floats(levels),
            floats(steps),
            floats(steps, 2),
            dma((7,)),
            dma((steps,)),
            dma((steps, 2)),
            dma((steps, 2)),
            dma((steps, 2)),
            dma((steps, 2)),
            dma((steps,)),
            dma((steps,)),
        ],
        compiler_params=pltpu.CompilerParams(collective_id=0, has_side_effects=True),
        name="coupled_window",
    )(state, prev, mixing, velocity, coupling, sea_mask, index, weight)


def solution(mesh):
    in_specs = (
        P("comp", None, "lat", "lon"),
        P(None, "lat", "lon"),
        P("comp", None, "lat", "lon"),
        P("comp", None, "lat", "lon"),
        P("comp", "lat", "lon"),
        P("comp", "lat", "lon"),
        P("comp", None, "lat", "lon"),
        P("comp", None, "lat", "lon"),
    )
    out_specs = (P("comp", None, "lat", "lon"), P("comp", None, "lat", "lon"))
    return jax.shard_map(
        functools.partial(per_device, mesh.shape["lat"], mesh.shape["lon"]),
        mesh=mesh,
        in_specs=in_specs,
        out_specs=out_specs,
        check_vma=False,
    )
```

time: 179 us -> 16.7 us (0.09); the launches traced: 177 us -> 16.5 us
  local copies, waits for them, and re-layouts: 140 us -> 2.15 us
  starting transfers between devices: 32 us -> 0 us
  Pallas kernels: 0 us -> 13.7 us
  other arithmetic: 2.96 us -> 0 us
    gather x6 -> x0, local copies, waits for them, and re-layouts: 137 us -> none  [regrid_local(): jnp.take(flat, index.reshape(index.shape[0], -1), axis=0)]
    ppermute x14 -> x0, starting transfers between devices: 32 us -> none  [the longest x6 13.6 us: extended(): after = lax.ppermute(initial, axis, down)]
    pallas_call x0 -> x1, Pallas kernels: none -> 13.7 us  [per_device(): pl.pallas_call(functools.partial(kernel, (n_lat, n_lon, steps, levels, ro...]
  transfers between devices with their start and end apart: 14 -> 0, of which waited for: 0 -> 0; matrix products, arithmetic and copies ran while one was open for 77% -> 0% of each run, Pallas kernels for 0% -> 0%
where the time goes in v1:
time: 16.7 us; the launch traced here: 16.5 us
  Pallas kernels  13.7 us (82%)
  local copies, waits for them, and re-layouts  2.15 us (13%)
  between operations  0.65 us (4%)
    pallas_call x1, Pallas kernels, per_device(): pl.pallas_call(functools.partial(kernel, (n_lat, n_lon, steps, levels, ro...  13.7 us
    unnamed x4, local copies, waits for them, and re-layouts  2.15 us

profile of v1, /device:TPU:0, one launch (start us, length us, event | category | flops | bytes accessed | tf_op | source)
XLA Modules:
  0.0 16.5 jit_solution(11540997147426706080)
XLA Ops:
  0.6 13.7 %coupled_window.1 = (f32[1,12,16,128]{3,2,1,0:T(8,128)}, f32[1,2,16,128]{3,2,1,0:T(8,128)}) custom-call(f32[1,12,16,128]{3,2,1,0:T(8,128)} %state.1, f32[2,16,128]{2,1,0:T(8,128)} %prev.1, f32[1,11,16,128]{3,2,1,0:T(8,128)} %mixing.1, f32[1,2,16,128]{3,2,1,0:T(8,128)} %velocity.1, f32[1,16,128]{2,1,0:T(8,128)} %coupling.1, s32[1,16,128]{2,1,0:T(8,128)} %sea_mask.1, ...), custom_call_target="tpu_custom_call" | custom-call | tf_op jit(solution)/shard_map/coupled_window/pallas_call | solution.py:338
  14.3 0.0 copy-start
  14.3 1.5 %copy.12 = f32[1,12,16,128]{3,2,1,0:T(8,128)} copy(f32[1,12,16,128]{3,2,1,0:T(8,128)} %get-tuple-element.4) | data formatting | bytes 196608
  15.9 0.0 copy-done
  15.9 0.6 %copy.13 = f32[1,2,16,128]{3,2,1,0:T(8,128)} copy(f32[1,2,16,128]{3,2,1,0:T(8,128)S(1)} %copy-done) | data formatting | bytes 32768
Async XLA Ops:
  14.3 1.6 %copy-start = (f32[1,2,16,128]{3,2,1,0:T(8,128)S(1)}, f32[1,2,16,128]{3,2,1,0:T(8,128)}, u32[]{:S(2)}) copy-start(f32[1,2,16,128]{3,2,1,0:T(8,128)} %get-tuple-element.5) | copy-start | bytes 49156

commit v2 on v1

--- a/solution.py
+++ b/solution.py
@@ -71,6 +71,10 @@
     lon_recv,
     flux_send,
     flux_recv,
+    result,
+    top,
+    out_sem,
+    top_sem,
 ):
     n_lat, n_lon, steps, levels, rows, cols = sizes
     comp, lat, lon = (lax.axis_index(a) for a in ("comp", "lat", "lon"))
@@ -118,6 +122,9 @@
         to_east.append(remote(lon_out.at[s], lon_in.at[s, 1], lon_send.at[s, 1], lon_recv.at[s, 1], east))
         to_ocean.append(remote(flux.at[s], src.at[s], flux_send.at[s], flux_recv.at[s], partner))
 
+    results = [pltpu.make_async_copy(result.at[i], new_state.at[0, i], out_sem.at[i]) for i in range(levels)]
+    tops = [pltpu.make_async_copy(top.at[s], series.at[0, s], top_sem.at[s]) for s in range(steps)]
+
     barrier = pltpu.get_barrier_semaphore()
 
     @pl.when(has_before)
@@ -164,6 +171,22 @@
     def _():
         ext[:, :, halo_high, :] = nothing
 
+    edges = has_before.astype(jnp.int32) + has_after.astype(jnp.int32)
+    pl.semaphore_wait(barrier, 2 + edges + is_atmosphere.astype(jnp.int32))
+
+    def send_halo(s):
+        @pl.when(has_before)
+        def _():
+            to_before[s].start()
+
+        @pl.when(has_after)
+        def _():
+            to_after[s].start()
+
+        to_west[s].start()
+        to_east[s].start()
+
+    send_halo(0)
     for copy in loads[1:5]:
         copy.wait()
     rate = cpl[...] * sea[...].astype(jnp.float32)
@@ -171,29 +194,8 @@
     @pl.when(is_atmosphere)
     def _():
         sources[0].wait()
-        part[0] = regrid(src.at[0], idx, wgt)
-        flux[0] = rate * (part[0] - ext[0, 0, own, :])
-
-    edges = has_before.astype(jnp.int32) + has_after.astype(jnp.int32)
-    pl.semaphore_wait(barrier, 2 + edges + is_atmosphere.astype(jnp.int32))
-
-    def send_halo(s):
-        @pl.when(has_before)
-        def _():
-            to_before[s].start()
-
-        @pl.when(has_after)
-        def _():
-            to_after[s].start()
-
-        to_west[s].start()
-        to_east[s].start()
-
-    @pl.when(is_atmosphere)
-    def _():
+        flux[0] = rate * (regrid(src.at[0], idx, wgt) - ext[0, 0, own, :])
         to_ocean[0].start()
-
-    send_halo(0)
 
     loads[5].wait()
     loads[6].wait()
@@ -286,12 +288,10 @@
             forcing = rate * regrid(src.at[s], idx, wgt)
             part[s] = forcing
 
-        if s == 0:
-            forcing = jnp.where(is_atmosphere, flux[0], part[0])
-        else:
-            forcing = jnp.where(is_atmosphere, flux[s], part[s])
+        forcing = jnp.where(is_atmosphere, flux[s], part[s])
         x = (y[0] + forcing) * inverse[0]
-        series[0, s] = jnp.where(is_atmosphere, forcing, x)
+        top[s] = jnp.where(is_atmosphere, forcing, x)
+        tops[s].start()
         last = s + 1 == steps
         if not last:
 
@@ -304,7 +304,8 @@
             if level > 0:
                 x = values[level] + ratio[level] * x
             if last:
-                new_state[0, level] = x
+                result[level] = x
+                results[level].start()
             else:
                 ext[s + 1, level, own, :] = x
         if not last:
@@ -327,6 +328,20 @@
 
         to_west[s].wait_send()
         to_east[s].wait_send()
+
+    for copy in tops + results:
+        copy.wait()
+
+
+def hand_over(state_in, series_in, state_out, series_out, sem):
+    copies = [
+        pltpu.make_async_copy(series_in, series_out, sem.at[0]),
+        pltpu.make_async_copy(state_in, state_out, sem.at[1]),
+    ]
+    for copy in copies:
+        copy.start()
+    for copy in copies:
+        copy.wait()
 
 
 def per_device(n_lat, n_lon, state, prev, mixing, velocity, coupling, sea_mask, index, weight):
@@ -335,14 +350,15 @@
     tile = (rows, cols)
     floats = lambda *lead: pltpu.VMEM(lead + tile, jnp.float32)
     dma = pltpu.SemaphoreType.DMA
-    return pl.pallas_call(
+    shapes = (
+        jax.ShapeDtypeStruct(state.shape, jnp.float32),
+        jax.ShapeDtypeStruct((1, steps) + tile, jnp.float32),
+    )
+    outs = pl.pallas_call(
         functools.partial(kernel, (n_lat, n_lon, steps, levels, rows, cols)),
-        out_shape=(
-            jax.ShapeDtypeStruct(state.shape, jnp.float32),
-            jax.ShapeDtypeStruct((1, steps) + tile, jnp.float32),
-        ),
-        in_specs=[pl.BlockSpec(memory_space=pltpu.HBM)] * 8,
-        out_specs=[pl.BlockSpec(memory_space=pltpu.VMEM)] * 2,
+        out_shape=shapes,
+        in_specs=[pl.BlockSpec(memory_space=pl.ANY)] * 8,
+        out_specs=[pl.BlockSpec(memory_space=pl.ANY)] * 2,
         scratch_shapes=[
             pltpu.VMEM((steps, levels, rows + 2 * PAD, cols), jnp.float32),
             floats(steps),
@@ -365,10 +381,22 @@
             dma((steps, 2)),
             dma((steps,)),
             dma((steps,)),
+            floats(levels),
+            floats(steps),
+            dma((levels,)),
+            dma((steps,)),
         ],
         compiler_params=pltpu.CompilerParams(collective_id=0, has_side_effects=True),
         name="coupled_window",
     )(state, prev, mixing, velocity, coupling, sea_mask, index, weight)
+    return pl.pallas_call(
+        hand_over,
+        out_shape=shapes,
+        in_specs=[pl.BlockSpec(memory_space=pl.ANY)] * 2,
+        out_specs=[pl.BlockSpec(memory_space=pl.ANY)] * 2,
+        scratch_shapes=[dma((2,))],
+        name="hand_over",
+    )(*outs)
 
 
 def solution(mesh):

time: 16.7 us -> 19.2 us (1.15)
  Pallas kernels: 13.7 us -> 18.4 us
  local copies, waits for them, and re-layouts: 2.15 us -> 0 us
    pallas_call x0 -> x1, Pallas kernels: none -> 4.59 us  [per_device(): pl.pallas_call(hand_over, out_shape=shapes, in_specs=[pl.BlockSpec(memory...]
    unnamed x4 -> x0, local copies, waits for them, and re-layouts: 2.15 us -> none
where the time goes in v2:
time: 19.2 us; the launch traced here: 19 us
  Pallas kernels  18.4 us (96%)
  between operations  0.64 us (3%)
    pallas_call x1, Pallas kernels, per_device(): pl.pallas_call(functools.partial(kernel, (n_lat, n_lon, steps, levels, ro...  13.8 us
    pallas_call x1, Pallas kernels, per_device(): pl.pallas_call(hand_over, out_shape=shapes, in_specs=[pl.BlockSpec(memory...  4.59 us

profile of v2, /device:TPU:0, one launch (start us, length us, event | category | flops | bytes accessed | tf_op | source)
XLA Modules:
  0.0 19.0 jit_solution(15393348061953701249)
XLA Ops:
  0.6 13.8 %coupled_window.1 = (f32[1,12,16,128]{3,2,1,0:T(8,128)}, f32[1,2,16,128]{3,2,1,0:T(8,128)}) custom-call(f32[1,12,16,128]{3,2,1,0:T(8,128)} %state.1, f32[2,16,128]{2,1,0:T(8,128)} %prev.1, f32[1,11,16,128]{3,2,1,0:T(8,128)} %mixing.1, f32[1,2,16,128]{3,2,1,0:T(8,128)} %velocity.1, f32[1,16,128]{2,1,0:T(8,128)} %coupling.1, s32[1,16,128]{2,1,0:T(8,128)} %sea_mask.1, ...), custom_call_target="tpu_custom_call" | custom-call | tf_op jit(solution)/shard_map/coupled_window/pallas_call | solution.py:357
  14.4 4.6 %hand_over.1 = (f32[1,12,16,128]{3,2,1,0:T(8,128)}, f32[1,2,16,128]{3,2,1,0:T(8,128)}) custom-call(f32[1,12,16,128]{3,2,1,0:T(8,128)} %get-tuple-element.4.state_in, f32[1,2,16,128]{3,2,1,0:T(8,128)} %get-tuple-element.5.series_in), custom_call_target="tpu_custom_call" | custom-call | tf_op jit(solution)/shard_map/hand_over/pallas_call | solution.py:392

commit v3 on v2

--- a/solution.py
+++ b/solution.py
@@ -11,6 +11,8 @@
 MESH = pl.DeviceIdType.MESH
 PAD = 8
 REACH = 2
+VMEM_BYTES = 8 * 2**20
+GROUPS = 4
 SUB = 8
 
 
@@ -71,10 +73,6 @@
     lon_recv,
     flux_send,
     flux_recv,
-    result,
-    top,
-    out_sem,
-    top_sem,
 ):
     n_lat, n_lon, steps, levels, rows, cols = sizes
     comp, lat, lon = (lax.axis_index(a) for a in ("comp", "lat", "lon"))
@@ -121,9 +119,6 @@
         to_west.append(remote(lon_out.at[s], lon_in.at[s, 0], lon_send.at[s, 0], lon_recv.at[s, 0], west))
         to_east.append(remote(lon_out.at[s], lon_in.at[s, 1], lon_send.at[s, 1], lon_recv.at[s, 1], east))
         to_ocean.append(remote(flux.at[s], src.at[s], flux_send.at[s], flux_recv.at[s], partner))
-
-    results = [pltpu.make_async_copy(result.at[i], new_state.at[0, i], out_sem.at[i]) for i in range(levels)]
-    tops = [pltpu.make_async_copy(top.at[s], series.at[0, s], top_sem.at[s]) for s in range(steps)]
 
     barrier = pltpu.get_barrier_semaphore()
 
@@ -290,8 +285,7 @@
 
         forcing = jnp.where(is_atmosphere, flux[s], part[s])
         x = (y[0] + forcing) * inverse[0]
-        top[s] = jnp.where(is_atmosphere, forcing, x)
-        tops[s].start()
+        series[0, s] = jnp.where(is_atmosphere, forcing, x)
         last = s + 1 == steps
         if not last:
 
@@ -304,8 +298,7 @@
             if level > 0:
                 x = values[level] + ratio[level] * x
             if last:
-                result[level] = x
-                results[level].start()
+                new_state[0, level] = x
             else:
                 ext[s + 1, level, own, :] = x
         if not last:
@@ -329,15 +322,14 @@
         to_west[s].wait_send()
         to_east[s].wait_send()
 
-    for copy in tops + results:
-        copy.wait()
-
 
 def hand_over(state_in, series_in, state_out, series_out, sem):
-    copies = [
-        pltpu.make_async_copy(series_in, series_out, sem.at[0]),
-        pltpu.make_async_copy(state_in, state_out, sem.at[1]),
-    ]
+    levels = state_in.shape[1]
+    group = pl.cdiv(levels, GROUPS)
+    copies = [pltpu.make_async_copy(series_in, series_out, sem.at[GROUPS])]
+    for i, first in enumerate(range(0, levels, group)):
+        some = pl.ds(first, min(group, levels - first))
+        copies.append(pltpu.make_async_copy(state_in.at[0, some], state_out.at[0, some], sem.at[i]))
     for copy in copies:
         copy.start()
     for copy in copies:
@@ -356,9 +348,9 @@
     )
     outs = pl.pallas_call(
         functools.partial(kernel, (n_lat, n_lon, steps, levels, rows, cols)),
-        out_shape=shapes,
-        in_specs=[pl.BlockSpec(memory_space=pl.ANY)] * 8,
-        out_specs=[pl.BlockSpec(memory_space=pl.ANY)] * 2,
+        out_shape=tuple(pltpu.VMEM(s.shape, s.dtype) for s in shapes),
+        in_specs=[pl.BlockSpec(memory_space=pltpu.HBM)] * 8,
+        out_specs=[pl.BlockSpec(memory_space=pltpu.VMEM)] * 2,
         scratch_shapes=[
             pltpu.VMEM((steps, levels, rows + 2 * PAD, cols), jnp.float32),
             floats(steps),
@@ -381,20 +373,17 @@
             dma((steps, 2)),
             dma((steps,)),
             dma((steps,)),
-            floats(levels),
-            floats(steps),
-            dma((levels,)),
-            dma((steps,)),
         ],
-        compiler_params=pltpu.CompilerParams(collective_id=0, has_side_effects=True),
+        compiler_params=pltpu.CompilerParams(collective_id=0, has_side_effects=True, vmem_limit_bytes=VMEM_BYTES),
         name="coupled_window",
-    )(state, prev, mixing, velocity, coupling, sea_mask, index, weight)
+    )(*(pltpu.with_memory_space_constraint(a, pltpu.HBM) for a in (state, prev, mixing, velocity, coupling, sea_mask, index, weight)))
     return pl.pallas_call(
         hand_over,
         out_shape=shapes,
-        in_specs=[pl.BlockSpec(memory_space=pl.ANY)] * 2,
+        in_specs=[pl.BlockSpec(memory_space=pltpu.VMEM)] * 2,
         out_specs=[pl.BlockSpec(memory_space=pl.ANY)] * 2,
-        scratch_shapes=[dma((2,))],
+        scratch_shapes=[dma((GROUPS + 1,))],
+        compiler_params=pltpu.CompilerParams(vmem_limit_bytes=VMEM_BYTES),
         name="hand_over",
     )(*outs)
 

time: 19.2 us -> 14.5 us (0.76)
  Pallas kernels: 18.4 us -> 13.7 us
    pallas_call x1, Pallas kernels: 4.59 us -> 0.68 us  [per_device(): pl.pallas_call(hand_over, out_shape=shapes, in_specs=[pl.BlockSpec(memory...]
    pallas_call x1, Pallas kernels: 13.8 us -> 13.1 us  [per_device(): pl.pallas_call(functools.partial(kernel, (n_lat, n_lon, steps, levels, ro...]
where the time goes in v3:
time: 14.5 us; the launch traced here: 14.4 us
  Pallas kernels  13.7 us (94%)
  between operations  0.64 us (4%)
    pallas_call x1, Pallas kernels, per_device(): pl.pallas_call(functools.partial(kernel, (n_lat, n_lon, steps, levels, ro...  13.1 us
    pallas_call x1, Pallas kernels, per_device(): pl.pallas_call(hand_over, out_shape=shapes, in_specs=[pl.BlockSpec(memory...  0.68 us

profile of v3, /device:TPU:0, one launch (start us, length us, event | category | flops | bytes accessed | tf_op | source)
XLA Modules:
  0.0 14.4 jit_solution(1452890348946299799)
XLA Ops:
  0.6 13.1 %coupled_window.1 = (f32[1,12,16,128]{3,2,1,0:T(8,128)S(1)}, f32[1,2,16,128]{3,2,1,0:T(8,128)S(1)}) custom-call(f32[1,12,16,128]{3,2,1,0:T(8,128)} %state.1, f32[2,16,128]{2,1,0:T(8,128)} %prev.1, f32[1,11,16,128]{3,2,1,0:T(8,128)} %mixing.1, f32[1,2,16,128]{3,2,1,0:T(8,128)} %velocity.1, f32[1,16,128]{2,1,0:T(8,128)} %coupling.1, s32[1,16,128]{2,1,0:T(8,128)} %sea_mask.1, ...), custom_call_target="tpu_custom_call" | custom-call | tf_op jit(solution)/shard_map/coupled_window/pallas_call | solution.py:349
  13.7 0.7 %hand_over.1 = (f32[1,12,16,128]{3,2,1,0:T(8,128)}, f32[1,2,16,128]{3,2,1,0:T(8,128)}) custom-call(f32[1,12,16,128]{3,2,1,0:T(8,128)S(1)} %get-tuple-element.4.state_in, f32[1,2,16,128]{3,2,1,0:T(8,128)S(1)} %get-tuple-element.5.series_in), custom_call_target="tpu_custom_call" | custom-call | tf_op jit(solution)/shard_map/hand_over/pallas_call | solution.py:380

commit v4 on v3

--- a/solution.py
+++ b/solution.py
@@ -25,17 +25,15 @@
     shift = cols.bit_length() - 1
     parts = []
     for top in range(0, rows, SUB):
-        where = [index[j, top : top + SUB, :] for j in range(points)]
-        lanes = [lax.bitwise_and(w, cols - 1) for w in where]
-        owners = [lax.shift_right_logical(w, shift) for w in where]
-        picked = [jnp.zeros((SUB, cols), jnp.float32)] * points
-        for row in range(rows):
-            line = jnp.broadcast_to(source[row : row + 1, :], (SUB, cols))
-            for j in range(points):
-                picked[j] = jnp.where(owners[j] == row, lane_gather(line, lanes[j]), picked[j])
-        total = weight[0, top : top + SUB, :] * picked[0]
-        for j in range(1, points):
-            total = total + weight[j, top : top + SUB, :] * picked[j]
+        total = jnp.zeros((SUB, cols), jnp.float32)
+        for j in range(points):
+            where = index[j, top : top + SUB, :]
+            lanes, owner = lax.bitwise_and(where, cols - 1), lax.shift_right_logical(where, shift)
+            picked = jnp.zeros((SUB, cols), jnp.float32)
+            for row in range(rows):
+                line = jnp.broadcast_to(source[row : row + 1, :], (SUB, cols))
+                picked = jnp.where(owner == row, lane_gather(line, lanes), picked)
+            total = total + weight[j, top : top + SUB, :] * picked
         parts.append(total)
     return jnp.concatenate(parts, axis=0)
 
@@ -85,20 +83,18 @@
     partner = {"comp": 1 - comp}
     own = pl.ds(PAD, rows)
 
-    loads = [
-        pltpu.make_async_copy(a, b, in_sem.at[i])
-        for i, (a, b) in enumerate(
-            (
-                (state.at[0], ext.at[0, :, own, :]),
-                (interp_index.at[0], idx),
-                (interp_weight.at[0], wgt),
-                (coupling.at[0], cpl),
-                (sea_mask.at[0], sea),
-                (velocity.at[0], vel),
-                (mixing.at[0], mix),
-            )
-        )
+    def chunks(count):
+        size = pl.cdiv(count, GROUPS)
+        return [pl.ds(first, min(size, count - first)) for first in range(0, count, size)]
+
+    count = iter(range(3 * GROUPS + 1))
+    load = lambda a, b: pltpu.make_async_copy(a, b, in_sem.at[next(count)])
+    load_state = [load(state.at[0, c], ext.at[0, c, own, :]) for c in chunks(levels)]
+    load_regrid = [
+        load(a.at[0], b) for a, b in ((interp_index, idx), (interp_weight, wgt), (coupling, cpl), (sea_mask, sea))
     ]
+    load_rest = [load(velocity.at[0], vel)]
+    load_rest += [load(mixing.at[0, c], mix.at[c]) for c in chunks(levels - 1)]
     sources = [pltpu.make_async_copy(prev.at[s], src.at[s], src_sem.at[s]) for s in range(steps)]
 
     def remote(a, b, send, recv, device):
@@ -121,17 +117,18 @@
         to_ocean.append(remote(flux.at[s], src.at[s], flux_send.at[s], flux_recv.at[s], partner))
 
     barrier = pltpu.get_barrier_semaphore()
-
-    @pl.when(has_before)
-    def _():
-        pl.semaphore_signal(barrier, inc=1, device_id=before, device_id_type=MESH)
-
-    @pl.when(has_after)
-    def _():
-        pl.semaphore_signal(barrier, inc=1, device_id=after, device_id_type=MESH)
-
     for side in (west, east):
         pl.semaphore_signal(barrier, inc=1, device_id=side, device_id_type=MESH)
+    for copy in load_state:
+        copy.start()
+
+    @pl.when(has_before)
+    def _():
+        pl.semaphore_signal(barrier, inc=1, device_id=before, device_id_type=MESH)
+
+    @pl.when(has_after)
+    def _():
+        pl.semaphore_signal(barrier, inc=1, device_id=after, device_id_type=MESH)
 
     @pl.when(is_ocean)
     def _():
@@ -142,20 +139,21 @@
         for copy in sources:
             copy.start()
 
-    for copy in loads:
+    for copy in load_regrid + load_rest:
         copy.start()
 
     lane = lax.broadcasted_iota(jnp.int32, (rows, cols), 1)
 
-    def pack(s):
-        packed = jnp.zeros((rows, cols), jnp.float32)
-        for level in range(levels):
-            turned = pltpu.roll(ext[s, level, own, :], (4 * level + REACH) % cols, 1)
-            packed = jnp.where((lane >= 4 * level) & (lane < 4 * level + 4), turned, packed)
-        lon_out[s] = packed
-
-    loads[0].wait()
-    pack(0)
+    def pack(packed, level, x):
+        turned = pltpu.roll(x, (4 * level + REACH) % cols, 1)
+        return jnp.where((lane >= 4 * level) & (lane < 4 * level + 4), turned, packed)
+
+    for copy in load_state:
+        copy.wait()
+    packed = jnp.zeros((rows, cols), jnp.float32)
+    for level in range(levels):
+        packed = pack(packed, level, ext[0, level, own, :])
+    lon_out[0] = packed
     nothing = jnp.zeros((steps, levels, REACH, cols), jnp.float32)
 
     @pl.when(jnp.logical_not(has_before))
@@ -170,19 +168,19 @@
     pl.semaphore_wait(barrier, 2 + edges + is_atmosphere.astype(jnp.int32))
 
     def send_halo(s):
-        @pl.when(has_before)
-        def _():
-            to_before[s].start()
-
-        @pl.when(has_after)
-        def _():
-            to_after[s].start()
-
         to_west[s].start()
         to_east[s].start()
 
+        @pl.when(has_before)
+        def _():
+            to_before[s].start()
+
+        @pl.when(has_after)
+        def _():
+            to_after[s].start()
+
     send_halo(0)
-    for copy in loads[1:5]:
+    for copy in load_regrid:
         copy.wait()
     rate = cpl[...] * sea[...].astype(jnp.float32)
 
@@ -192,8 +190,8 @@
         flux[0] = rate * (regrid(src.at[0], idx, wgt) - ext[0, 0, own, :])
         to_ocean[0].start()
 
-    loads[5].wait()
-    loads[6].wait()
+    for copy in load_rest:
+        copy.wait()
     east_speed, north_speed = vel[0] * (1.0 / 12.0), vel[1] * (1.0 / 12.0)
     centre = 1.0 - 4.0 * SMOOTHING
     lon_m2, lon_m1 = -east_speed, SMOOTHING + 8.0 * east_speed
@@ -242,6 +240,11 @@
             def _():
                 sources[s + 1].wait()
                 part[s + 1] = regrid(src.at[s + 1], idx, wgt)
+
+        @pl.when(is_ocean)
+        def _():
+            to_ocean[s].wait_recv()
+            part[s] = rate * regrid(src.at[s], idx, wgt)
 
         @pl.when(has_after)
         def _():
@@ -277,12 +280,6 @@
             else:
                 y[0] = total
 
-        @pl.when(is_ocean)
-        def _():
-            to_ocean[s].wait_recv()
-            forcing = rate * regrid(src.at[s], idx, wgt)
-            part[s] = forcing
-
         forcing = jnp.where(is_atmosphere, flux[s], part[s])
         x = (y[0] + forcing) * inverse[0]
         series[0, s] = jnp.where(is_atmosphere, forcing, x)
@@ -294,6 +291,7 @@
                 flux[s + 1] = rate * (part[s + 1] - x)
                 to_ocean[s + 1].start()
 
+        packed = jnp.zeros((rows, cols), jnp.float32)
         for level in range(levels):
             if level > 0:
                 x = values[level] + ratio[level] * x
@@ -301,8 +299,9 @@
                 new_state[0, level] = x
             else:
                 ext[s + 1, level, own, :] = x
+                packed = pack(packed, level, x)
         if not last:
-            pack(s + 1)
+            lon_out[s + 1] = packed
             send_halo(s + 1)
 
     for s in range(steps):
@@ -365,7 +364,7 @@
             floats(levels),
             floats(steps),
             floats(steps, 2),
-            dma((7,)),
+            dma((3 * GROUPS + 1,)),
             dma((steps,)),
             dma((steps, 2)),
             dma((steps, 2)),

time: 14.5 us -> 14.6 us (level)
  no operation moved by 1% of the time
where the time goes in v4:
time: 14.6 us; the launch traced here: 14.4 us
  Pallas kernels  13.8 us (95%)
  between operations  0.64 us (4%)
    pallas_call x1, Pallas kernels, per_device(): pl.pallas_call(functools.partial(kernel, (n_lat, n_lon, steps, levels, ro...  13.1 us
    pallas_call x1, Pallas kernels, per_device(): pl.pallas_call(hand_over, out_shape=shapes, in_specs=[pl.BlockSpec(memory...  0.68 us

profile of v4, /device:TPU:0, one launch (start us, length us, event | category | flops | bytes accessed | tf_op | source)
XLA Modules:
  0.0 14.4 jit_solution(5393226075290610255)
XLA Ops:
  0.6 13.1 %coupled_window.1 = (f32[1,12,16,128]{3,2,1,0:T(8,128)S(1)}, f32[1,2,16,128]{3,2,1,0:T(8,128)S(1)}) custom-call(f32[1,12,16,128]{3,2,1,0:T(8,128)} %state.1, f32[2,16,128]{2,1,0:T(8,128)} %prev.1, f32[1,11,16,128]{3,2,1,0:T(8,128)} %mixing.1, f32[1,2,16,128]{3,2,1,0:T(8,128)} %velocity.1, f32[1,16,128]{2,1,0:T(8,128)} %coupling.1, s32[1,16,128]{2,1,0:T(8,128)} %sea_mask.1, ...), custom_call_target="tpu_custom_call" | custom-call | tf_op jit(solution)/shard_map/coupled_window/pallas_call | solution.py:348
  13.7 0.7 %hand_over.1 = (f32[1,12,16,128]{3,2,1,0:T(8,128)}, f32[1,2,16,128]{3,2,1,0:T(8,128)}) custom-call(f32[1,12,16,128]{3,2,1,0:T(8,128)S(1)} %get-tuple-element.4.state_in, f32[1,2,16,128]{3,2,1,0:T(8,128)S(1)} %get-tuple-element.5.series_in), custom_call_target="tpu_custom_call" | custom-call | tf_op jit(solution)/shard_map/hand_over/pallas_call | solution.py:379

commit v5 on v4

--- a/solution.py
+++ b/solution.py
@@ -61,6 +61,8 @@
     part,
     flux,
     y,
+    lat_out,
+    lat_in,
     lon_out,
     lon_in,
     in_sem,
@@ -102,16 +104,11 @@
             src_ref=a, dst_ref=b, send_sem=send, recv_sem=recv, device_id=device, device_id_type=MESH
         )
 
-    low, high = pl.ds(PAD, REACH), pl.ds(PAD + rows - REACH, REACH)
     halo_low, halo_high = pl.ds(PAD - REACH, REACH), pl.ds(PAD + rows, REACH)
     to_before, to_after, to_west, to_east, to_ocean = [], [], [], [], []
     for s in range(steps):
-        to_before.append(
-            remote(ext.at[s, :, low, :], ext.at[s, :, halo_high, :], lat_send.at[s, 0], lat_recv.at[s, 0], before)
-        )
-        to_after.append(
-            remote(ext.at[s, :, high, :], ext.at[s, :, halo_low, :], lat_send.at[s, 1], lat_recv.at[s, 1], after)
-        )
+        to_before.append(remote(lat_out.at[s, 0], lat_in.at[s, 0], lat_send.at[s, 0], lat_recv.at[s, 0], before))
+        to_after.append(remote(lat_out.at[s, 1], lat_in.at[s, 1], lat_send.at[s, 1], lat_recv.at[s, 1], after))
         to_west.append(remote(lon_out.at[s], lon_in.at[s, 0], lon_send.at[s, 0], lon_recv.at[s, 0], west))
         to_east.append(remote(lon_out.at[s], lon_in.at[s, 1], lon_send.at[s, 1], lon_recv.at[s, 1], east))
         to_ocean.append(remote(flux.at[s], src.at[s], flux_send.at[s], flux_recv.at[s], partner))
@@ -148,11 +145,17 @@
         turned = pltpu.roll(x, (4 * level + REACH) % cols, 1)
         return jnp.where((lane >= 4 * level) & (lane < 4 * level + 4), turned, packed)
 
+    def pack_lat(s, level, x):
+        lat_out[s, 0, pl.ds(REACH * level, REACH), :] = x[:REACH]
+        lat_out[s, 1, pl.ds(REACH * level, REACH), :] = x[rows - REACH :]
+
     for copy in load_state:
         copy.wait()
     packed = jnp.zeros((rows, cols), jnp.float32)
     for level in range(levels):
-        packed = pack(packed, level, ext[0, level, own, :])
+        x = ext[0, level, own, :]
+        packed = pack(packed, level, x)
+        pack_lat(0, level, x)
     lon_out[0] = packed
     nothing = jnp.zeros((steps, levels, REACH, cols), jnp.float32)
 
@@ -168,16 +171,16 @@
     pl.semaphore_wait(barrier, 2 + edges + is_atmosphere.astype(jnp.int32))
 
     def send_halo(s):
+        @pl.when(has_before)
+        def _():
+            to_before[s].start()
+
+        @pl.when(has_after)
+        def _():
+            to_after[s].start()
+
         to_west[s].start()
         to_east[s].start()
-
-        @pl.when(has_before)
-        def _():
-            to_before[s].start()
-
-        @pl.when(has_after)
-        def _():
-            to_after[s].start()
 
     send_halo(0)
     for copy in load_regrid:
@@ -249,10 +252,14 @@
         @pl.when(has_after)
         def _():
             to_before[s].wait_recv()
+            for level in range(levels):
+                ext[s, level, halo_high, :] = lat_in[s, 0, pl.ds(REACH * level, REACH), :]
 
         @pl.when(has_before)
         def _():
             to_after[s].wait_recv()
+            for level in range(levels):
+                ext[s, level, halo_low, :] = lat_in[s, 1, pl.ds(REACH * level, REACH), :]
 
         to_west[s].wait_recv()
         to_east[s].wait_recv()
@@ -300,6 +307,7 @@
             else:
                 ext[s + 1, level, own, :] = x
                 packed = pack(packed, level, x)
+                pack_lat(s + 1, level, x)
         if not last:
             lon_out[s + 1] = packed
             send_halo(s + 1)
@@ -362,6 +370,8 @@
             floats(steps),
             floats(steps),
             floats(levels),
+            pltpu.VMEM((steps, 2, levels * REACH, cols), jnp.float32),
+            pltpu.VMEM((steps, 2, levels * REACH, cols), jnp.float32),
             floats(steps),
             floats(steps, 2),
             dma((3 * GROUPS + 1,)),

time: 14.6 us -> 14.6 us (level)
  no operation moved by 1% of the time
where the time goes in v5:
time: 14.6 us; the launch traced here: 14.4 us
  Pallas kernels  13.8 us (95%)
  between operations  0.64 us (4%)
    pallas_call x1, Pallas kernels, per_device(): pl.pallas_call(functools.partial(kernel, (n_lat, n_lon, steps, levels, ro...  13.1 us
    pallas_call x1, Pallas kernels, per_device(): pl.pallas_call(hand_over, out_shape=shapes, in_specs=[pl.BlockSpec(memory...  0.68 us

profile of v5, /device:TPU:0, one launch (start us, length us, event | category | flops | bytes accessed | tf_op | source)
XLA Modules:
  0.0 14.4 jit_solution(883228068499696452)
XLA Ops:
  0.6 13.1 %coupled_window.1 = (f32[1,12,16,128]{3,2,1,0:T(8,128)S(1)}, f32[1,2,16,128]{3,2,1,0:T(8,128)S(1)}) custom-call(f32[1,12,16,128]{3,2,1,0:T(8,128)} %state.1, f32[2,16,128]{2,1,0:T(8,128)} %prev.1, f32[1,11,16,128]{3,2,1,0:T(8,128)} %mixing.1, f32[1,2,16,128]{3,2,1,0:T(8,128)} %velocity.1, f32[1,16,128]{2,1,0:T(8,128)} %coupling.1, s32[1,16,128]{2,1,0:T(8,128)} %sea_mask.1, ...), custom_call_target="tpu_custom_call" | custom-call | tf_op jit(solution)/shard_map/coupled_window/pallas_call | solution.py:356
  13.7 0.7 %hand_over.1 = (f32[1,12,16,128]{3,2,1,0:T(8,128)}, f32[1,2,16,128]{3,2,1,0:T(8,128)}) custom-call(f32[1,12,16,128]{3,2,1,0:T(8,128)S(1)} %get-tuple-element.4.state_in, f32[1,2,16,128]{3,2,1,0:T(8,128)S(1)} %get-tuple-element.5.series_in), custom_call_target="tpu_custom_call" | custom-call | tf_op jit(solution)/shard_map/hand_over/pallas_call | solution.py:389

commit v6 on v5

--- a/solution.py
+++ b/solution.py
@@ -237,13 +237,6 @@
 
     for s in range(steps):
         own_part(s)
-        if s + 1 < steps:
-
-            @pl.when(is_atmosphere)
-            def _():
-                sources[s + 1].wait()
-                part[s + 1] = regrid(src.at[s + 1], idx, wgt)
-
         @pl.when(is_ocean)
         def _():
             to_ocean[s].wait_recv()
@@ -291,13 +284,6 @@
         x = (y[0] + forcing) * inverse[0]
         series[0, s] = jnp.where(is_atmosphere, forcing, x)
         last = s + 1 == steps
-        if not last:
-
-            @pl.when(is_atmosphere)
-            def _():
-                flux[s + 1] = rate * (part[s + 1] - x)
-                to_ocean[s + 1].start()
-
         packed = jnp.zeros((rows, cols), jnp.float32)
         for level in range(levels):
             if level > 0:
@@ -311,6 +297,12 @@
         if not last:
             lon_out[s + 1] = packed
             send_halo(s + 1)
+
+            @pl.when(is_atmosphere)
+            def _():
+                sources[s + 1].wait()
+                flux[s + 1] = rate * (regrid(src.at[s + 1], idx, wgt) - ext[s + 1, 0, own, :])
+                to_ocean[s + 1].start()
 
     for s in range(steps):
 

time: 14.6 us -> 14.6 us (level)
  no operation moved by 1% of the time
where the time goes in v6:
time: 14.6 us; the launch traced here: 14.4 us
  Pallas kernels  13.7 us (94%)
  between operations  0.64 us (4%)
    pallas_call x1, Pallas kernels, per_device(): pl.pallas_call(functools.partial(kernel, (n_lat, n_lon, steps, levels, ro...  13.1 us
    pallas_call x1, Pallas kernels, per_device(): pl.pallas_call(hand_over, out_shape=shapes, in_specs=[pl.BlockSpec(memory...  0.68 us

profile of v6, /device:TPU:0, one launch (start us, length us, event | category | flops | bytes accessed | tf_op | source)
XLA Modules:
  0.0 14.4 jit_solution(2654520499541562182)
XLA Ops:
  0.6 13.1 %coupled_window.1 = (f32[1,12,16,128]{3,2,1,0:T(8,128)S(1)}, f32[1,2,16,128]{3,2,1,0:T(8,128)S(1)}) custom-call(f32[1,12,16,128]{3,2,1,0:T(8,128)} %state.1, f32[2,16,128]{2,1,0:T(8,128)} %prev.1, f32[1,11,16,128]{3,2,1,0:T(8,128)} %mixing.1, f32[1,2,16,128]{3,2,1,0:T(8,128)} %velocity.1, f32[1,16,128]{2,1,0:T(8,128)} %coupling.1, s32[1,16,128]{2,1,0:T(8,128)} %sea_mask.1, ...), custom_call_target="tpu_custom_call" | custom-call | tf_op jit(solution)/shard_map/coupled_window/pallas_call | solution.py:348
  13.7 0.7 %hand_over.1 = (f32[1,12,16,128]{3,2,1,0:T(8,128)}, f32[1,2,16,128]{3,2,1,0:T(8,128)}) custom-call(f32[1,12,16,128]{3,2,1,0:T(8,128)S(1)} %get-tuple-element.4.state_in, f32[1,2,16,128]{3,2,1,0:T(8,128)S(1)} %get-tuple-element.5.series_in), custom_call_target="tpu_custom_call" | custom-call | tf_op jit(solution)/shard_map/hand_over/pallas_call | solution.py:381

commit v7 on v5

--- a/solution.py
+++ b/solution.py
@@ -85,18 +85,14 @@
     partner = {"comp": 1 - comp}
     own = pl.ds(PAD, rows)
 
-    def chunks(count):
-        size = pl.cdiv(count, GROUPS)
-        return [pl.ds(first, min(size, count - first)) for first in range(0, count, size)]
-
-    count = iter(range(3 * GROUPS + 1))
+    count = iter(range(7))
     load = lambda a, b: pltpu.make_async_copy(a, b, in_sem.at[next(count)])
-    load_state = [load(state.at[0, c], ext.at[0, c, own, :]) for c in chunks(levels)]
+    load_state = [load(state.at[0], ext.at[0, :, own, :])]
     load_regrid = [
         load(a.at[0], b) for a, b in ((interp_index, idx), (interp_weight, wgt), (coupling, cpl), (sea_mask, sea))
     ]
     load_rest = [load(velocity.at[0], vel)]
-    load_rest += [load(mixing.at[0, c], mix.at[c]) for c in chunks(levels - 1)]
+    load_rest += [load(mixing.at[0], mix)]
     sources = [pltpu.make_async_copy(prev.at[s], src.at[s], src_sem.at[s]) for s in range(steps)]
 
     def remote(a, b, send, recv, device):
@@ -223,6 +219,7 @@
         inverse[level] = 1.0 / pivot
         if level > 0:
             ratio[level] = mix[level - 1] * inverse[level]
+    carry = [mix[level] * inverse[level] for level in range(levels - 1)]
 
     def own_part(s):
         for level in range(levels):
@@ -280,15 +277,12 @@
                 + lat_p2 * ext[s, level, pl.ds(PAD + 2, rows), :]
                 + jnp.where(on_rim, pltpu.roll(rims, (cols - REACH - 4 * level) % cols, 1), 0.0)
             )
+            values[level] = total * inverse[level]
             if level < levels - 1:
-                total = total + mix[level] * values[level + 1]
-            if level > 0:
-                values[level] = total * inverse[level]
-            else:
-                y[0] = total
+                values[level] = values[level] + carry[level] * values[level + 1]
 
         forcing = jnp.where(is_atmosphere, flux[s], part[s])
-        x = (y[0] + forcing) * inverse[0]
+        x = values[0] + forcing * inverse[0]
         series[0, s] = jnp.where(is_atmosphere, forcing, x)
         last = s + 1 == steps
         if not last:
@@ -374,7 +368,7 @@
             pltpu.VMEM((steps, 2, levels * REACH, cols), jnp.float32),
             floats(steps),
             floats(steps, 2),
-            dma((3 * GROUPS + 1,)),
+            dma((7,)),
             dma((steps,)),
             dma((steps, 2)),
             dma((steps, 2)),

time: 14.6 us -> 14.5 us (level)
  no operation moved by 1% of the time
where the time goes in v7:
time: 14.5 us; the launch traced here: 14.3 us
  Pallas kernels  13.7 us (94%)
  between operations  0.64 us (4%)
    pallas_call x1, Pallas kernels, per_device(): pl.pallas_call(functools.partial(kernel, (n_lat, n_lon, steps, levels, ro...  13 us
    pallas_call x1, Pallas kernels, per_device(): pl.pallas_call(hand_over, out_shape=shapes, in_specs=[pl.BlockSpec(memory...  0.68 us

profile of v7, /device:TPU:0, one launch (start us, length us, event | category | flops | bytes accessed | tf_op | source)
XLA Modules:
  0.0 14.3 jit_solution(6535288236357865444)
XLA Ops:
  0.6 13.0 %coupled_window.1 = (f32[1,12,16,128]{3,2,1,0:T(8,128)S(1)}, f32[1,2,16,128]{3,2,1,0:T(8,128)S(1)}) custom-call(f32[1,12,16,128]{3,2,1,0:T(8,128)} %state.1, f32[2,16,128]{2,1,0:T(8,128)} %prev.1, f32[1,11,16,128]{3,2,1,0:T(8,128)} %mixing.1, f32[1,2,16,128]{3,2,1,0:T(8,128)} %velocity.1, f32[1,16,128]{2,1,0:T(8,128)} %coupling.1, s32[1,16,128]{2,1,0:T(8,128)} %sea_mask.1, ...), custom_call_target="tpu_custom_call" | custom-call | tf_op jit(solution)/shard_map/coupled_window/pallas_call | solution.py:350
  13.6 0.7 %hand_over.1 = (f32[1,12,16,128]{3,2,1,0:T(8,128)}, f32[1,2,16,128]{3,2,1,0:T(8,128)}) custom-call(f32[1,12,16,128]{3,2,1,0:T(8,128)S(1)} %get-tuple-element.4.state_in, f32[1,2,16,128]{3,2,1,0:T(8,128)S(1)} %get-tuple-element.5.series_in), custom_call_target="tpu_custom_call" | custom-call | tf_op jit(solution)/shard_map/hand_over/pallas_call | solution.py:383

commit v8 on v7

--- a/solution.py
+++ b/solution.py
@@ -103,8 +103,14 @@
     halo_low, halo_high = pl.ds(PAD - REACH, REACH), pl.ds(PAD + rows, REACH)
     to_before, to_after, to_west, to_east, to_ocean = [], [], [], [], []
     for s in range(steps):
-        to_before.append(remote(lat_out.at[s, 0], lat_in.at[s, 0], lat_send.at[s, 0], lat_recv.at[s, 0], before))
-        to_after.append(remote(lat_out.at[s, 1], lat_in.at[s, 1], lat_send.at[s, 1], lat_recv.at[s, 1], after))
+        if s == 0:
+            rows_low = (state.at[0, :, pl.ds(0, REACH), :], ext.at[0, :, halo_high, :])
+            rows_high = (state.at[0, :, pl.ds(rows - REACH, REACH), :], ext.at[0, :, halo_low, :])
+        else:
+            rows_low = (lat_out.at[s, 0], lat_in.at[s, 0])
+            rows_high = (lat_out.at[s, 1], lat_in.at[s, 1])
+        to_before.append(remote(*rows_low, lat_send.at[s, 0], lat_recv.at[s, 0], before))
+        to_after.append(remote(*rows_high, lat_send.at[s, 1], lat_recv.at[s, 1], after))
         to_west.append(remote(lon_out.at[s], lon_in.at[s, 0], lon_send.at[s, 0], lon_recv.at[s, 0], west))
         to_east.append(remote(lon_out.at[s], lon_in.at[s, 1], lon_send.at[s, 1], lon_recv.at[s, 1], east))
         to_ocean.append(remote(flux.at[s], src.at[s], flux_send.at[s], flux_recv.at[s], partner))
@@ -145,13 +151,29 @@
         lat_out[s, 0, pl.ds(REACH * level, REACH), :] = x[:REACH]
         lat_out[s, 1, pl.ds(REACH * level, REACH), :] = x[rows - REACH :]
 
+    edges = has_before.astype(jnp.int32) + has_after.astype(jnp.int32)
+    pl.semaphore_wait(barrier, 2 + edges + is_atmosphere.astype(jnp.int32))
+
+    def send_lat(s):
+        @pl.when(has_before)
+        def _():
+            to_before[s].start()
+
+        @pl.when(has_after)
+        def _():
+            to_after[s].start()
+
+    def send_lon(s):
+        to_west[s].start()
+        to_east[s].start()
+
+    send_lat(0)
     for copy in load_state:
         copy.wait()
     packed = jnp.zeros((rows, cols), jnp.float32)
     for level in range(levels):
         x = ext[0, level, own, :]
         packed = pack(packed, level, x)
-        pack_lat(0, level, x)
     lon_out[0] = packed
     nothing = jnp.zeros((steps, levels, REACH, cols), jnp.float32)
 
@@ -163,22 +185,7 @@
     def _():
         ext[:, :, halo_high, :] = nothing
 
-    edges = has_before.astype(jnp.int32) + has_after.astype(jnp.int32)
-    pl.semaphore_wait(barrier, 2 + edges + is_atmosphere.astype(jnp.int32))
-
-    def send_halo(s):
-        @pl.when(has_before)
-        def _():
-            to_before[s].start()
-
-        @pl.when(has_after)
-        def _():
-            to_after[s].start()
-
-        to_west[s].start()
-        to_east[s].start()
-
-    send_halo(0)
+    send_lon(0)
     for copy in load_regrid:
         copy.wait()
     rate = cpl[...] * sea[...].astype(jnp.float32)
@@ -249,13 +256,13 @@
         @pl.when(has_after)
         def _():
             to_before[s].wait_recv()
-            for level in range(levels):
+            for level in range(levels if s > 0 else 0):
                 ext[s, level, halo_high, :] = lat_in[s, 0, pl.ds(REACH * level, REACH), :]
 
         @pl.when(has_before)
         def _():
             to_after[s].wait_recv()
-            for level in range(levels):
+            for level in range(levels if s > 0 else 0):
                 ext[s, level, halo_low, :] = lat_in[s, 1, pl.ds(REACH * level, REACH), :]
 
         to_west[s].wait_recv()
@@ -304,7 +311,8 @@
                 pack_lat(s + 1, level, x)
         if not last:
             lon_out[s + 1] = packed
-            send_halo(s + 1)
+            send_lat(s + 1)
+            send_lon(s + 1)
 
     for s in range(steps):
 

time: 14.5 us -> 14.6 us (level)
  no operation moved by 1% of the time
where the time goes in v8:
time: 14.6 us; the launch traced here: 14.4 us
  Pallas kernels  13.8 us (95%)
  between operations  0.64 us (4%)
    pallas_call x1, Pallas kernels, per_device(): pl.pallas_call(functools.partial(kernel, (n_lat, n_lon, steps, levels, ro...  13.1 us
    pallas_call x1, Pallas kernels, per_device(): pl.pallas_call(hand_over, out_shape=shapes, in_specs=[pl.BlockSpec(memory...  0.68 us

profile of v8, /device:TPU:0, one launch (start us, length us, event | category | flops | bytes accessed | tf_op | source)
XLA Modules:
  0.0 14.4 jit_solution(10388773968403304131)
XLA Ops:
  0.6 13.1 %coupled_window.1 = (f32[1,12,16,128]{3,2,1,0:T(8,128)S(1)}, f32[1,2,16,128]{3,2,1,0:T(8,128)S(1)}) custom-call(f32[1,12,16,128]{3,2,1,0:T(8,128)} %state.1, f32[2,16,128]{2,1,0:T(8,128)} %prev.1, f32[1,11,16,128]{3,2,1,0:T(8,128)} %mixing.1, f32[1,2,16,128]{3,2,1,0:T(8,128)} %velocity.1, f32[1,16,128]{2,1,0:T(8,128)} %coupling.1, s32[1,16,128]{2,1,0:T(8,128)} %sea_mask.1, ...), custom_call_target="tpu_custom_call" | custom-call | tf_op jit(solution)/shard_map/coupled_window/pallas_call | solution.py:358
  13.7 0.7 %hand_over.1 = (f32[1,12,16,128]{3,2,1,0:T(8,128)}, f32[1,2,16,128]{3,2,1,0:T(8,128)}) custom-call(f32[1,12,16,128]{3,2,1,0:T(8,128)S(1)} %get-tuple-element.4.state_in, f32[1,2,16,128]{3,2,1,0:T(8,128)S(1)} %get-tuple-element.5.series_in), custom_call_target="tpu_custom_call" | custom-call | tf_op jit(solution)/shard_map/hand_over/pallas_call | solution.py:391
